TPU v7x, 32 devices: a whole 2x2x4 slice. The times are simulated.
32 devices in a mesh: grp: 4 (over z), rve: 8 (over y, x, core).
Axes of the slice: x: 2, y: 2, z: 4, core: 2. Of those that a mesh axis runs over, the one named last changes fastest.
Arguments:
- displacement: float32 [3, 64, 32, 128], P(None, ('grp', 'rve')), may hold values from -6 to 6
- stiffness: bfloat16 [27, 3, 3, 64, 32, 128], P(None, None, None, ('grp', 'rve')), may hold values from -0.65625 to 0.65625
- external: float32 [3, 64, 32, 128], P(None, ('grp', 'rve')), may hold values from -6 to 6
- point_node: int32 [8], P('grp'), may hold values from 0 to 65535
- point_owner: int32 [8, 1], P('grp'), may hold values from 0 to 3; in each aligned block of 2 rows (0 to 1, 2 to 3, ...) no two rows name the same one
- point_load: float32 [8, 18], P('grp'), may hold values from -6 to 6
- moduli_diag: float32 [4, 6, 8, 64, 128], P('grp', None, 'rve'), may hold values from 1.5 to 4
- moduli_off: float32 [4, 36, 8, 64, 128], P('grp', None, 'rve'), may hold values from -1 to 1
- schmid: float32 [4, 72, 8, 64, 128], P('grp', None, 'rve'), may hold values from -1 to 1
- crss: float32 [4, 12, 8, 64, 128], P('grp', None, 'rve'), may hold values from 0.3 to 3
- branch: int32 [4, 8, 64, 128], P('grp', 'rve'), may hold values from 0 to 4095
- rate: float32 [4, 8, 64, 128], P('grp', 'rve'), may hold values from 0.03 to 0.3
Outputs:
- residual: float32 [3, 64, 32, 128], P(None, ('grp', 'rve'))
- point_stress: float32 [8, 6], P('grp')
Inputs may be any that keep to these rules, and one draw needn't show every extreme that they name: `point_owner`: among the 2 points of one quarter's list, at most 1 name the same volume, a bound that some block reaches.
All inputs are finite; a program needn't handle non-finite values.
Results may differ from a plain program's by a relative error of at most 0.0003.
Values sent between devices are 32-bit elements; how exact they have to be, the bound alone decides.
A program may use at most 128 MiB of HBM per device.

v0:
```python
import functools
import jax
import jax.numpy as jnp
from jax import lax
from jax.experimental import pallas as pl
from jax.experimental.pallas import tpu as pltpu
from jax.sharding import PartitionSpec as P

MESH = pl.DeviceIdType.MESH

SLIP = 12
SWEEPS = 10


RELAX = 0.15
NEIGHBOUR_WEIGHT = 1.0 / 6.0


def padded_2(value, sides, width, wrap):
    for axis, dim in sides:
        count, length = (lax.axis_size(axis), value.shape[dim])
        up = [(i, (i + 1) % count) for i in range(count if wrap else count - 1)]
        down = [(j, i) for i, j in up]
        last = lax.slice_in_dim(value, length - width, length, axis=dim)
        first = lax.slice_in_dim(value, 0, width, axis=dim)
        before = lax.ppermute(last, axis, up)
        after = lax.ppermute(first, axis, down)
        value = jnp.concatenate([before, value, after], axis=dim)
    return value


def stiff_apply(blocks, padded):
    extent = (padded.shape[1] - 2, padded.shape[2] - 2, padded.shape[3] - 2)
    summed = jnp.zeros((3,) + extent, jnp.float32)
    for i in range(3):
        for j in range(3):
            for k in range(3):
                offset = i * 9 + j * 3 + k
                window = padded[:, i : i + extent[0], j : j + extent[1], k : k + extent[2]]
                summed = summed + jnp.sum(blocks[offset].astype(jnp.float32) * window[None], axis=1)
    return summed


def node_strain(padded):
    extent = (padded.shape[1] - 2, padded.shape[2] - 2, padded.shape[3] - 2)

    def gradient(c, k):
        lower = [slice(1, 1 + extent[0]), slice(1, 1 + extent[1]), slice(1, 1 + extent[2])]
        upper = list(lower)
        lower[k] = slice(0, extent[k])
        upper[k] = slice(2, 2 + extent[k])
        return (padded[c][tuple(upper)] - padded[c][tuple(lower)]) * 0.5

    table = [[gradient(c, k) for k in range(3)] for c in range(3)]
    return jnp.stack(
        [
            table[0][0],
            table[1][1],
            table[2][2],
            table[1][2] + table[2][1],
            table[0][2] + table[2][0],
            table[0][1] + table[1][0],
        ]
    )


def activity(branch):
    bit_index = jnp.arange(SLIP, dtype=jnp.int32)
    return (jnp.right_shift(branch[None], bit_index[:, None, None, None]) & 1).astype(jnp.float32)


def elastic_matrix(diagonal, offdiag):
    return (
        offdiag.reshape((6, 6) + offdiag.shape[1:])
        + jnp.eye(6, dtype=jnp.float32)[:, :, None, None, None] * diagonal[None]
    )


def make_entry(diagonal, offdiag, schmid_rows, critical, plastic_rate):
    matrix = elastic_matrix(diagonal, offdiag)
    schmid_mat = schmid_rows.reshape((12, 6) + schmid_rows.shape[1:])
    return (
        matrix,
        schmid_mat,
        critical[:, None],
        plastic_rate[:, None],
        jnp.swapaxes(schmid_mat, 0, 1),
    )


def contract(matrix, field):
    summed = matrix[:, 0][:, None] * field[0][None]
    for j in range(1, matrix.shape[1]):
        summed = summed + matrix[:, j][:, None] * field[j][None]
    return summed


def sweeps(ebar, entry, plane_sum):
    baseline = ebar[:, :, None, None, None]
    matrix, schmid_mat, critical, plastic_rate, schmid_back = entry
    shape = (6, ebar.shape[1]) + matrix.shape[2:]
    fluctuation = jnp.zeros(shape, jnp.float32)
    plastic = jnp.zeros(shape, jnp.float32)
    for sweep in range(SWEEPS):
        strain = baseline + fluctuation - plastic
        stress = contract(matrix, strain)
        resolved = contract(schmid_mat, stress)
        slipped = plastic_rate * (resolved - critical * jnp.tanh(resolved / critical))
        plastic = plastic + contract(schmid_back, slipped)
        beside = (
            plane_sum(strain, stress) + jnp.roll(stress, 1, axis=3) + jnp.roll(stress, -1, axis=3)
        )
        beside = beside + jnp.roll(stress, 1, axis=4) + jnp.roll(stress, -1, axis=4)
        fluctuation = fluctuation - RELAX * (stress - NEIGHBOUR_WEIGHT * beside)
    final_strain = baseline + fluctuation - plastic
    return contract(matrix, final_strain)


def ring_place(index):
    high, low = index // 4, index % 4
    return 4 * high + 2 * ((low // 2 + high) % 2) + low % 2


def volume_kernel(
    members,
    ebar,
    diag,
    off,
    schmid,
    crss,
    branch,
    rate,
    out,
    diag_v,
    off_v,
    schmid_v,
    crss_v,
    branch_v,
    rate_v,
    strain_v,
    stress_v,
    edge_v,
    halo_v,
    send_sems,
    recv_sems,
    local_sems,
    edge_send,
    edge_recv,
):
    me = lax.axis_index("rve")
    place = ring_place(me)
    sources = [off, diag, schmid, crss, branch, rate]
    targets = [off_v, diag_v, schmid_v, crss_v, branch_v, rate_v]
    barrier = pltpu.get_barrier_semaphore()
    for k in range(1, members):
        pl.semaphore_signal(
            barrier, inc=1, device_id={"rve": (me + k) % members}, device_id_type=MESH
        )
    pl.semaphore_wait(barrier, members - 1)

    def block_of(source, device):
        rows = pl.ds(pl.multiple_of(ring_place(device) * 8, 8), 8)
        return source.at[0, :, 0, rows, :]

    copies = []
    for n in range(6):
        for k in range(1, members):
            peer = (me + k) % members
            copy = pltpu.make_async_remote_copy(
                src_ref=block_of(sources[n], peer),
                dst_ref=targets[n].at[me],
                send_sem=send_sems.at[n, k],
                recv_sem=recv_sems.at[n, k],
                device_id={"rve": peer},
                device_id_type=MESH,
            )
            copy.start()
            copies.append(copy)
        local = pltpu.make_async_copy(
            block_of(sources[n], me), targets[n].at[me], local_sems.at[n]
        )
        local.start()
        copies.append(local)
    for copy in copies:
        copy.wait()

    def prepare(v, carry):
        for i in range(6):
            off_v[v, 7 * i] = off_v[v, 7 * i] + diag_v[v, i]
        bits, speed = branch_v[v, 0], rate_v[v, 0]
        for a in range(SLIP):
            critical = crss_v[v, a]
            inverse = 1.0 / critical
            for i in range(6):
                schmid_v[v, 6 * a + i] = schmid_v[v, 6 * a + i] * inverse
            active = ((bits >> a) & 1).astype(jnp.float32)
            crss_v[v, a] = active * speed * (critical * critical)
        for p in range(points):
            for i in range(6):
                strain_v[v, 6 * p + i] = jnp.full((8, 128), ebar[p, i], jnp.float32)
        return carry

    points = ebar.shape[0]
    parts = 6 * points
    lax.fori_loop(0, members, prepare, 0)

    def elastic(v, strain):
        stress = []
        for i in range(6):
            sums = [None] * points
            for j in range(6):
                c = off_v[v, 6 * i + j]
                for p in range(points):
                    term = c * strain[6 * p + j]
                    sums[p] = term if j == 0 else sums[p] + term
            stress.append(sums)
        return [stress[i][p] for p in range(points) for i in range(6)]

    def keep(v, now, stress):
        for k in range(parts):
            stress_v[now, v, k] = stress[k]
            edge_v[now, 0, v, k : k + 1, :] = stress[k][7:8, :]
            edge_v[now, 1, v, k : k + 1, :] = stress[k][0:1, :]

    def first(v, carry):
        keep(v, 0, elastic(v, [strain_v[v, k] for k in range(parts)]))
        return carry

    lax.fori_loop(0, members, first, 0)
    following = ring_place((place + 1) % members)
    previous = ring_place((place + members - 1) % members)
    row = lax.broadcasted_iota(jnp.int32, (8, 128), 0)
    top, bottom = row == 0, row == 7

    def edge_copy(now, way):
        return pltpu.make_async_remote_copy(
            src_ref=edge_v.at[now, way],
            dst_ref=halo_v.at[now, way],
            send_sem=edge_send.at[now, way],
            recv_sem=edge_recv.at[now, way],
            device_id={"rve": following if way == 0 else previous},
            device_id_type=MESH,
        )

    def slip(now, v):
        for half in range(0, points, 2):
            pair = range(half, min(half + 2, points))
            stress = {(p, i): stress_v[now, v, 6 * p + i] for p in pair for i in range(6)}
            change = {}
            for a in range(SLIP):
                rows = [schmid_v[v, 6 * a + i] for i in range(6)]
                weight = crss_v[v, a]
                for p in pair:
                    ratio = rows[0] * stress[p, 0]
                    for i in range(1, 6):
                        ratio = ratio + rows[i] * stress[p, i]
                    slipped = weight * (ratio - jnp.tanh(ratio))
                    for i in range(6):
                        term = rows[i] * slipped
                        change[p, i] = term if a == 0 else change[p, i] + term
            for p in pair:
                for i in range(6):
                    strain_v[v, 6 * p + i] = strain_v[v, 6 * p + i] - change[p, i]

    def advance(now, v):
        before, after = (v + members - 1) % members, (v + 1) % members
        strain = []
        for k in range(parts):
            stress = stress_v[now, v, k]
            above = jnp.where(top, halo_v[now, 0, v, k : k + 1, :], pltpu.roll(stress, 1, 0))
            below = jnp.where(bottom, halo_v[now, 1, v, k : k + 1, :], pltpu.roll(stress, 7, 0))
            beside = (stress_v[now, before, k] + stress_v[now, after, k]) + (above + below)
            beside = beside + (pltpu.roll(stress, 1, 1) + pltpu.roll(stress, 127, 1))
            value = strain_v[v, k] - RELAX * (stress - NEIGHBOUR_WEIGHT * beside)
            strain_v[v, k] = value
            strain.append(value)
        keep(v, 1 - now, elastic(v, strain))

    def sweep(s, carry):
        now = s % 2
        edges = [edge_copy(now, way) for way in range(2)]
        for copy in edges:
            copy.start()

        def slip_plane(v, inner):
            slip(now, v)
            return inner

        def advance_plane(v, inner):
            advance(now, v)
            return inner

        lax.fori_loop(0, members, slip_plane, 0)
        for copy in edges:
            copy.wait()
        lax.fori_loop(0, members, advance_plane, 0)
        return carry

    lax.fori_loop(0, SWEEPS, sweep, 0)
    last = SWEEPS % 2
    for k in range(parts):
        total = stress_v[last, 0, k]
        for v in range(1, members):
            total = total + stress_v[last, v, k]
        out[k] = total


def volume_sums(ebar, diag, off, schmid, crss, branch, rate):
    members = lax.axis_size("rve")
    points = ebar.shape[0]
    any_space = pl.BlockSpec(memory_space=pl.ANY)

    def held(count, dtype=jnp.float32):
        return pltpu.VMEM((members, count, 8, 128), dtype)

    parts = 6 * points
    sums = pl.pallas_call(
        functools.partial(volume_kernel, members),
        out_shape=jax.ShapeDtypeStruct((parts, 8, 128), jnp.float32),
        in_specs=[pl.BlockSpec(memory_space=pltpu.SMEM)] + [any_space] * 6,
        out_specs=pl.BlockSpec(memory_space=pltpu.VMEM),
        scratch_shapes=[
            held(6),
            held(36),
            held(72),
            held(12),
            held(1, jnp.int32),
            held(1),
            held(parts),
            pltpu.VMEM((2, members, parts, 8, 128), jnp.float32),
            pltpu.VMEM((2, 2, members, parts, 128), jnp.float32),
            pltpu.VMEM((2, 2, members, parts, 128), jnp.float32),
            pltpu.SemaphoreType.DMA((6, members)),
            pltpu.SemaphoreType.DMA((6, members)),
            pltpu.SemaphoreType.DMA((6,)),
            pltpu.SemaphoreType.DMA((2, 2)),
            pltpu.SemaphoreType.DMA((2, 2)),
        ],
        compiler_params=pltpu.CompilerParams(
            collective_id=0, has_side_effects=True, vmem_limit_bytes=40 * 1024 * 1024
        ),
        cost_estimate=pl.CostEstimate(
            flops=20 * 180 * parts * members * 1024, bytes_accessed=8 << 20, transcendentals=0
        ),
    )(ebar, diag, off, schmid, crss, branch[None], rate[None])
    return jnp.sum(sums, axis=(1, 2))


def plane_sums(ebar, moduli_diag, moduli_off, schmid, crss, branch, rate):
    plastic_rate = activity(branch[0]) * rate[0]
    entry = make_entry(moduli_diag[0], moduli_off[0], schmid[0], crss[0], plastic_rate)

    def plane_sum(strain, stress):
        rimmed = padded_2(stress, (("rve", 2),), 1, True)
        return rimmed[:, :, :-2] + rimmed[:, :, 2:]

    final = sweeps(ebar, entry, plane_sum)
    return jnp.sum(final, axis=(2, 3, 4))


def per_device(
    displacement,
    stiffness,
    external,
    point_node,
    point_owner,
    point_load,
    moduli_diag,
    moduli_off,
    schmid,
    crss,
    branch,
    rate,
):
    extended = padded_2(displacement, ((("grp", "rve"), 1),), 1, False)
    padded = jnp.pad(extended, ((0, 0), (0, 0), (1, 1), (1, 1)))
    applied = stiff_apply(stiffness, padded)
    strain_field = node_strain(padded).reshape(6, -1)
    groups = lax.axis_size("grp")
    members = lax.axis_size("rve")
    member = lax.axis_index("rve")
    local_nodes = strain_field.shape[1]
    shifted_node = point_node - member * local_nodes
    present = ((shifted_node >= 0) & (shifted_node < local_nodes)).astype(jnp.float32)
    safe_node = jnp.clip(shifted_node, 0, local_nodes - 1)
    partial_value = strain_field[:, safe_node].T * present[:, None]
    count = point_owner.shape[0]
    capacity = count // 2
    owner = point_owner[:, 0]
    onehot = (owner[:, None] == jnp.arange(groups, dtype=jnp.int32)[None, :]).astype(jnp.float32)
    ranked = jnp.cumsum(onehot, axis=0) - onehot
    slot_of = jnp.sum(ranked * onehot, axis=1)
    slot_match = (
        slot_of[None, None, :] == jnp.arange(capacity, dtype=jnp.float32)[None, :, None]
    ).astype(jnp.float32)
    select = onehot.T[:, None, :] * slot_match
    quarter = lax.psum(partial_value, "rve")
    outgoing = jnp.einsum("gsp,pi->gsi", select, quarter, precision=lax.Precision.HIGHEST)
    arrived = lax.all_to_all(outgoing, "grp", split_axis=0, concat_axis=0, tiled=True)
    ebar = arrived.reshape(-1, 6).T
    voxels = members * rate.shape[1] * rate.shape[2] * rate.shape[3]
    if members == 8 and rate.shape[1:] == (1, 64, 128):
        local_sums = volume_sums(ebar.T, moduli_diag, moduli_off, schmid, crss, branch, rate)
        local_sums = local_sums.reshape(-1, 6).T
    else:
        local_sums = plane_sums(ebar, moduli_diag, moduli_off, schmid, crss, branch, rate)
    totals = lax.psum(local_sums, "rve") / voxels
    returned = lax.all_to_all(
        jnp.transpose(totals.reshape(6, groups, capacity), (1, 2, 0)),
        "grp",
        split_axis=0,
        concat_axis=0,
        tiled=True,
    )
    point_stress = jnp.einsum("gsp,gsi->pi", select, returned, precision=lax.Precision.HIGHEST)
    force = jnp.einsum(
        "pcj,pj->pc", point_load.reshape(-1, 3, 6), point_stress, precision=lax.Precision.HIGHEST
    )
    flat = (external - applied).reshape(3, -1).at[:, safe_node].add(-(force * present[:, None]).T)
    return (flat.reshape(external.shape), point_stress)


def solution(mesh):
    in_specs = (
        P(None, ("grp", "rve"), None, None),
        P(None, None, None, ("grp", "rve"), None, None),
        P(None, ("grp", "rve"), None, None),
        P("grp"),
        P("grp", None),
        P("grp", None),
        P("grp", None, "rve", None, None),
        P("grp", None, "rve", None, None),
        P("grp", None, "rve", None, None),
        P("grp", None, "rve", None, None),
        P("grp", "rve", None, None),
        P("grp", "rve", None, None),
    )
    out_specs = (P(None, ("grp", "rve"), None, None), P("grp", None))
    return jax.shard_map(
        per_device, mesh=mesh, in_specs=in_specs, out_specs=out_specs, check_vma=False
    )
```

profile of v0, /device:TPU:0, one launch (start us, length us, event | category | flops | bytes accessed | tf_op | source)
XLA Modules:
  0.0 180.5 jit_solution(2032068946188852617)
XLA Ops:
  0.6 0.8 fusion.60
  1.5 2.3 %collective-permute-start = (f32[3,1,32,128]{3,2,1,0:T(8,128)S(1)}, f32[3,1,32,128]{3,2,1,0:T(8,128)S(1)}, u32[]{:S(2)}, u32[]{:S(2)}) collective-permute-start(f32[3,1,32,128]{3,2,1,0:T(8,128)S(1)} %get-tuple-element.72), channel_id=1, source_target_pairs={{0,1},{1,2},{2,3},{3,4},{4,5},{5,6},{6,7},{7,8},{8,9},{9,10},{10,1... | collective-permute-start | bytes 147464 | tf_op jit(solution)/shard_map/ppermute | solution.py:26
  3.8 1.3 collective-permute-start.1
  7.2 0.8 select_reduce_fusion
  9.1 1.1 select_maximum_fusion
  10.7 2.6 %copy.30 = f32[6,8192]{0,1:T(8,128)} copy(f32[6,8192]{1,0:T(8,128)S(1)} %stack.27) | data formatting | bytes 393216 | tf_op jit(solution)/shard_map/stack | solution.py:55
  13.4 2.7 %gather_fusion = f32[2,6]{1,0:T(2,128)S(1)} fusion(f32[6,8192]{0,1:T(8,128)} %copy.30, s32[1024]{0:T(1024)S(1)} %pad_clamp_fusion), kind=kCustom, calls=%fused_computation | custom fusion | bytes 104 | tf_op jit(solution)/shard_map/gather | solution.py:386
  16.2 1.5 fusion.58
  17.7 18.4 %psum.14 = f32[2,6]{1,0:T(2,128)S(1)} all-reduce(f32[2,6]{1,0:T(2,128)S(1)} %broadcast_multiply_fusion.1), channel_id=1, replica_groups=mesh['grp'=4,'rve'=8] {'rve'}, use_global_device_ids=true, to_apply=%region_29.30 | all-reduce | flops 12 | bytes 96 | tf_op jit(solution)/shard_map/psum | solution.py:397
  36.8 3.9 %all-to-all-start = ((f32[4,1,6]{2,1,0:T(1,128)}), f32[4,1,6]{2,1,0:T(1,128)S(1)}, u32[]{:S(2)}, u32[]{:S(2)}) async-start(f32[4,1,6]{2,1,0:T(1,128)} %bitcast.40), calls=%async_computation | async-start | bytes 4096 | tf_op jit(solution)/shard_map/all_to_all | solution.py:399
  40.9 3.1 %fusion.29 = (f32[3,2,32,128]{3,2,1,0:T(8,128)}, f32[3,2,32,128]{3,2,1,0:T(8,128)}, f32[3,2,32,128]{3,2,1,0:T(8,128)}, f32[3,2,32,128]{3,2,1,0:T(8,128)}, f32[3,...) fusion(f32[3,2,32,128]{3,2,1,0:T(8,128)S(1)} %get-tuple-element, ...), kind=kLoop, calls=%fused_computation.64 | loop fusion | flops 1769472 | bytes 3096576 | tf_op jit(solution)/shard_map/reduce_sum | solution.py:40
  44.1 2.4 %fusion.27 = (f32[3,2,32,128]{3,2,1,0:T(8,128)}, f32[3,2,32,128]{3,2,1,0:T(8,128)}, f32[3,2,32,128]{3,2,1,0:T(8,128)}, f32[3,2,32,128]{3,2,1,0:T(8,128)}, f32[3,...) fusion(f32[3,2,32,128]{3,2,1,0:T(8,128)S(1)} %get-tuple-element, ...), kind=kLoop, calls=%fused_computation.60 | loop fusion | flops 1769472 | bytes 3096576 | tf_op jit(solution)/shard_map/reduce_sum | solution.py:40
  46.6 1.2 fusion.28
  47.8 1.0 copy-done.3
  48.8 0.9 copy-done.4
  51.2 94.9 %shard_map.131 = f32[24,8,128]{2,1,0:T(8,128)S(1)} custom-call(f32[4,6]{1,0:T(4,128)S(1)} %bitcast.123, f32[1,6,1,64,128]{4,3,2,1,0:T(8,128)S(1)} %copy-done.4, f32[1,36,1,64,128]{4,3,2,1,0:T(8,128)S(1)} %copy-done.1, f32[1,72,1,64,128]{4,3,2,1,0:T(8,128)S(1)} %copy-done, f32[1,12,1,64,128]{4,3,2,1,0:T(8,128)S(1)} %copy-done.3, ...), custom_call_target="tpu_custom_call" | custom-call | flops 707788800 | bytes 8388608 | tf_op jit(solution)/shard_map/pallas_call | solution.py:317
  146.8 1.2 reduce_sum.289
  148.0 12.7 %psum.15 = f32[6,4]{0,1:T(4,128)S(1)} all-reduce(f32[6,4]{0,1:T(4,128)S(1)} %bitcast.132), channel_id=1, replica_groups=mesh['grp'=4,'rve'=8] {'rve'}, use_global_device_ids=true, to_apply=%region_31.32 | all-reduce | flops 24 | bytes 192 | tf_op jit(solution)/shard_map/psum | solution.py:407
  161.3 5.1 %all-to-all-start.1 = ((f32[4,1,6]{2,1,0:T(1,128)}), f32[4,1,6]{2,1,0:T(1,128)S(1)}, u32[]{:S(2)}, u32[]{:S(2)}) async-start(f32[4,1,6]{2,1,0:T(1,128)} %bitcast.47), calls=%async_computation.1 | async-start | bytes 4096 | tf_op jit(solution)/shard_map/all_to_all | solution.py:408
  166.4 2.1 %add_subtract_fusion = f32[3,2,32,128]{3,2,1,0:T(8,128)S(1)} fusion(f32[3,2,32,128]{3,2,1,0:T(8,128)} %param.14, f32[3,2,32,128]{3,2,1,0:T(8,128)} %get-tuple-element.35, f32[3,2,32,128]{3,2,1,0:T(8,128)} %get-tuple-element.36, f32[3,2,32,128]{3,2,1,0:T(8,128)} %get-tuple-element.11, f32[3,2,32,128]{3,2,1,0:T(8,128)} %get-tuple-element.12, ...), kind=kLoop, calls=%fused_computation.70 | loop fusion | flops 663552 | bytes 2850816 | tf_op jit(solution)/shard_map/sub | solution.py:419
  168.4 2.6 %copy.29 = f32[3,2,32,128]{0,3,2,1:T(8,128)} copy(f32[3,2,32,128]{3,2,1,0:T(8,128)S(1)} %add_subtract_fusion) | data formatting | bytes 196608 | tf_op jit(solution)/shard_map/sub | solution.py:419
  171.0 0.9 all-to-all-done.1
  172.2 4.7 %scatter_custom_fusion = f32[3,8192]{0,1:T(8,128)} fusion(f32[3,8192]{0,1:T(8,128)} %bitcast.124, s32[2]{0:T(128)S(1)} %compare_select_fusion, f32[2,3]{1,0:T(2,128)S(1)} %bitcast.134, f32[2]{0:T(128)S(1)} %and_convert_fusion), kind=kCustom, calls=%fused_computation.99 | custom fusion | flops 18 | bytes 99840 | tf_op jit(solution)/shard_map/scatter-add | solution.py:419
  177.0 3.5 %copy.33 = f32[3,2,32,128]{3,2,1,0:T(8,128)} copy(f32[3,2,32,128]{0,3,2,1:T(8,128)} %bitcast.125) | data formatting | bytes 196608
  (60 shorter events, 7.8 us)
Async XLA Ops:
  1.5 7.4 %collective-permute-start = (f32[3,1,32,128]{3,2,1,0:T(8,128)S(1)}, f32[3,1,32,128]{3,2,1,0:T(8,128)S(1)}, u32[]{:S(2)}, u32[]{:S(2)}) collective-permute-start(f32[3,1,32,128]{3,2,1,0:T(8,128)S(1)} %get-tuple-element.72), channel_id=1, source_target_pairs={{0,1},{1,2},{2,3},{3,4},{4,5},{5,6},{6,7},{7,8},{8,9},{9,10},{10,1... | collective-permute-start | bytes 147464 | tf_op jit(solution)/shard_map/ppermute | solution.py:26
  3.8 5.2 %collective-permute-start.1 = (f32[3,1,32,128]{3,2,1,0:T(8,128)S(1)}, f32[3,1,32,128]{3,2,1,0:T(8,128)S(1)}, u32[]{:S(2)}, u32[]{:S(2)}) collective-permute-start(f32[3,1,32,128]{3,2,1,0:T(8,128)S(1)} %get-tuple-element.73), channel_id=1, source_target_pairs={{1,0},{2,1},{3,2},{4,3},{5,4},{6,5},{7,6},{8,7},{9,8},{10,9},{11,1... | collective-permute-start | bytes 147464 | tf_op jit(solution)/shard_map/ppermute | solution.py:27
  8.1 28.1 %copy-start.18 = (f32[2]{0:T(128)}, f32[2]{0:T(128)S(1)}, u32[]{:S(2)}) copy-start(f32[2]{0:T(128)S(1)} %compare_convert_fusion) | copy-start | bytes 28
  10.7 25.4 %copy-start.16 = (s32[2,1]{0,1:T(1,128)S(1)}, s32[2,1]{0,1:T(1,128)}, u32[]{:S(2)}) copy-start(s32[2,1]{0,1:T(1,128)} %param.16) | copy-start | bytes 28
  10.7 30.0 %copy-start.8 = (f32[3,2,32,128]{3,2,1,0:T(8,128)S(1)}, f32[3,2,32,128]{3,2,1,0:T(8,128)}, u32[]{:S(2)}) copy-start(f32[3,2,32,128]{3,2,1,0:T(8,128)} %param.12) | copy-start | bytes 294916
  36.8 10.9 %all-to-all-start = ((f32[4,1,6]{2,1,0:T(1,128)}), f32[4,1,6]{2,1,0:T(1,128)S(1)}, u32[]{:S(2)}, u32[]{:S(2)}) async-start(f32[4,1,6]{2,1,0:T(1,128)} %bitcast.40), calls=%async_computation | async-start | bytes 4096 | tf_op jit(solution)/shard_map/all_to_all | solution.py:399
  40.7 3.4 %copy-start.7 = (bf16[27,3,3,2,32,128]{5,4,3,2,1,0:T(8,128)(2,1)S(1)}, bf16[27,3,3,2,32,128]{5,4,3,2,1,0:T(8,128)(2,1)}, u32[]{:S(2)}) copy-start(bf16[27,3,3,2,32,128]{5,4,3,2,1,0:T(8,128)(2,1)} %param.13) | copy-start | bytes 11943940
  40.7 5.8 %copy-start.9 = (f32[3,2,32,128]{3,2,1,0:T(8,128)S(1)}, f32[3,2,32,128]{3,2,1,0:T(8,128)}, u32[]{:S(2)}) copy-start(f32[3,2,32,128]{3,2,1,0:T(8,128)} %get-tuple-element.43) | copy-start | bytes 294916
  40.7 5.8 %copy-start.10 = (f32[3,2,32,128]{3,2,1,0:T(8,128)S(1)}, f32[3,2,32,128]{3,2,1,0:T(8,128)}, u32[]{:S(2)}) copy-start(f32[3,2,32,128]{3,2,1,0:T(8,128)} %get-tuple-element.44) | copy-start | bytes 294916
  40.7 5.8 %copy-start.11 = (f32[3,2,32,128]{3,2,1,0:T(8,128)S(1)}, f32[3,2,32,128]{3,2,1,0:T(8,128)}, u32[]{:S(2)}) copy-start(f32[3,2,32,128]{3,2,1,0:T(8,128)} %get-tuple-element.45) | copy-start | bytes 294916
  40.7 5.8 %copy-start.12 = (f32[3,2,32,128]{3,2,1,0:T(8,128)S(1)}, f32[3,2,32,128]{3,2,1,0:T(8,128)}, u32[]{:S(2)}) copy-start(f32[3,2,32,128]{3,2,1,0:T(8,128)} %get-tuple-element.46) | copy-start | bytes 294916
  40.7 5.8 %copy-start.13 = (f32[3,2,32,128]{3,2,1,0:T(8,128)S(1)}, f32[3,2,32,128]{3,2,1,0:T(8,128)}, u32[]{:S(2)}) copy-start(f32[3,2,32,128]{3,2,1,0:T(8,128)} %get-tuple-element.47) | copy-start | bytes 294916
  40.7 5.8 %copy-start.14 = (f32[3,2,32,128]{3,2,1,0:T(8,128)S(1)}, f32[3,2,32,128]{3,2,1,0:T(8,128)}, u32[]{:S(2)}) copy-start(f32[3,2,32,128]{3,2,1,0:T(8,128)} %get-tuple-element.48) | copy-start | bytes 294916
  40.8 5.8 %copy-start.15 = (f32[3,2,32,128]{3,2,1,0:T(8,128)S(1)}, f32[3,2,32,128]{3,2,1,0:T(8,128)}, u32[]{:S(2)}) copy-start(f32[3,2,32,128]{3,2,1,0:T(8,128)} %get-tuple-element.49) | copy-start | bytes 294916
  40.9 6.8 %copy-start = (f32[1,72,1,64,128]{4,3,2,1,0:T(8,128)S(1)}, f32[1,72,1,64,128]{4,3,2,1,0:T(8,128)}, u32[]{:S(2)}) copy-start(f32[1,72,1,64,128]{4,3,2,1,0:T(8,128)} %schmid.1) | copy-start | bytes 7077892
  40.9 6.8 %copy-start.1 = (f32[1,36,1,64,128]{4,3,2,1,0:T(8,128)S(1)}, f32[1,36,1,64,128]{4,3,2,1,0:T(8,128)}, u32[]{:S(2)}) copy-start(f32[1,36,1,64,128]{4,3,2,1,0:T(8,128)} %off.1) | copy-start | bytes 3538948
  47.8 1.0 copy-start.3
  48.8 0.9 copy-start.4
  49.7 0.8 copy-start.5
  50.4 0.8 copy-start.6
  146.8 25.2 %copy-start.17 = (s32[2,1]{0,1:T(1,128)S(1)}, s32[2,1]{0,1:T(1,128)}, u32[]{:S(2)}) copy-start(s32[2,1]{0,1:T(1,128)} %param.16) | copy-start | bytes 28
  146.8 25.2 %copy-start.19 = (f32[2]{0:T(128)S(1)}, f32[2]{0:T(128)}, u32[]{:S(2)}) copy-start(f32[2]{0:T(128)} %copy-done.18) | copy-start | bytes 28
  161.3 10.6 %all-to-all-start.1 = ((f32[4,1,6]{2,1,0:T(1,128)}), f32[4,1,6]{2,1,0:T(1,128)S(1)}, u32[]{:S(2)}, u32[]{:S(2)}) async-start(f32[4,1,6]{2,1,0:T(1,128)} %bitcast.47), calls=%async_computation.1 | async-start | bytes 4096 | tf_op jit(solution)/shard_map/all_to_all | solution.py:408
  172.1 8.4 %copy-start.20 = (f32[2,6]{1,0:T(2,128)}, f32[2,6]{1,0:T(2,128)S(1)}, u32[]{:S(2)}) copy-start(f32[2,6]{1,0:T(2,128)S(1)} %fusion.42) | copy-start | bytes 148
  (1 other events, 0.6 us)
where the time goes:
time: 181 us; the launch traced here: 180 us
  Pallas kernels  94.9 us (52%)
  blocking collectives  31.1 us (17%)
  other arithmetic  19.8 us (11%)
  local copies, waits for them, and re-layouts  19.1 us (11%)
  starting transfers between devices  12.6 us (7%)
    pallas_call x1, Pallas kernels, volume_sums(): pl.pallas_call(functools.partial(volume_kernel, members), out_shape=jax.S...  94.9 us
    psum x1, blocking collectives, per_device(): quarter = lax.psum(partial_value, 'rve')  18.4 us
    psum x1, blocking collectives, per_device(): totals = lax.psum(local_sums, 'rve') / voxels  12.7 us
    unnamed x43, local copies, waits for them, and re-layouts  7.6 us
    reduce_sum x3, other arithmetic, stiff_apply(): jnp.sum(blocks[offset].astype(jnp.float32) * window[None], axis=1)  6.75 us
    all_to_all x1, starting transfers between devices, per_device(): lax.all_to_all(jnp.transpose(totals.reshape(6, groups, capacity), (1, 2,...  5.09 us
    scatter-add x1, other arithmetic, per_device(): (external - applied).reshape(3, -1).at[:, safe_node]  4.75 us
    all_to_all x1, starting transfers between devices, per_device(): lax.all_to_all(outgoing, 'grp', split_axis=0, concat_axis=0, tiled=True)  3.86 us
  transfers between devices with their start and end apart: 4, of which 2 were waited for; matrix products, arithmetic and copies ran while one was open for 8% of the time, Pallas kernels for 0%

commit v1 on v0

--- a/solution.py
+++ b/solution.py
@@ -7,6 +7,7 @@
 from jax.sharding import PartitionSpec as P
 
 MESH = pl.DeviceIdType.MESH
+CHUNK = 2
 
 SLIP = 12
 SWEEPS = 10
@@ -123,14 +124,21 @@
 
 def volume_kernel(
     members,
-    ebar,
+    groups,
+    displacement,
+    stiffness,
+    external,
+    node,
+    owner,
+    load,
     diag,
     off,
     schmid,
     crss,
     branch,
     rate,
-    out,
+    residual,
+    point_stress,
     diag_v,
     off_v,
     schmid_v,
@@ -141,68 +149,224 @@
     stress_v,
     edge_v,
     halo_v,
+    stiff_v,
+    extended_v,
+    shifted_v,
+    own_part,
+    all_parts,
+    own_total,
+    all_totals,
+    own_sum,
+    all_sums,
+    own_back,
+    all_back,
     send_sems,
     recv_sems,
     local_sems,
     edge_send,
     edge_recv,
+    layer_send,
+    layer_recv,
+    member_send,
+    member_recv,
+    group_send,
+    group_recv,
 ):
-    me = lax.axis_index("rve")
+    points = groups
+    parts = 6 * points
+    listed = node.shape[0]
+    me, mine = lax.axis_index("rve"), lax.axis_index("grp")
+    linear, devices = mine * members + me, groups * members
     place = ring_place(me)
     sources = [off, diag, schmid, crss, branch, rate]
     targets = [off_v, diag_v, schmid_v, crss_v, branch_v, rate_v]
+
+    def slab_part(number):
+        number = number % devices
+        return {"grp": number // members, "rve": number % members}
+
     barrier = pltpu.get_barrier_semaphore()
-    for k in range(1, members):
-        pl.semaphore_signal(
-            barrier, inc=1, device_id={"rve": (me + k) % members}, device_id_type=MESH
+    greeted = [{"rve": (me + k) % members} for k in range(1, members)]
+    greeted += [{"grp": (mine + k) % groups} for k in range(1, groups)]
+    greeted += [slab_part(linear + 1), slab_part(linear + devices - 1)]
+    for device in greeted:
+        pl.semaphore_signal(barrier, inc=1, device_id=device, device_id_type=MESH)
+    pl.semaphore_wait(barrier, len(greeted))
+
+    layers = []
+    for way in range(2):
+        layers.append(
+            pltpu.make_async_remote_copy(
+                src_ref=displacement.at[:, 1 - way],
+                dst_ref=extended_v.at[:, 3 * way],
+                send_sem=layer_send.at[way],
+                recv_sem=layer_recv.at[way],
+                device_id=slab_part(linear + (1 if way == 0 else devices - 1)),
+                device_id_type=MESH,
+            )
         )
-    pl.semaphore_wait(barrier, members - 1)
+        layers[way].start()
+    stiff_copy = pltpu.make_async_copy(stiffness, stiff_v, local_sems.at[6])
+    stiff_copy.start()
 
     def block_of(source, device):
         rows = pl.ds(pl.multiple_of(ring_place(device) * 8, 8), 8)
         return source.at[0, :, 0, rows, :]
 
-    copies = []
-    for n in range(6):
+    def start_blocks(which):
+        copies = []
+        for n in which:
+            for k in range(1, members):
+                peer = (me + k) % members
+                copies.append(
+                    pltpu.make_async_remote_copy(
+                        src_ref=block_of(sources[n], peer),
+                        dst_ref=targets[n].at[me],
+                        send_sem=send_sems.at[n, k],
+                        recv_sem=recv_sems.at[n, k],
+                        device_id={"rve": peer},
+                        device_id_type=MESH,
+                    )
+                )
+                copies[-1].start()
+            copies.append(
+                pltpu.make_async_copy(
+                    block_of(sources[n], me), targets[n].at[me], local_sems.at[n]
+                )
+            )
+            copies[-1].start()
+        return copies
+
+    def to_members(stage, source, target):
+        target[me] = source[...]
+        copies = []
         for k in range(1, members):
-            peer = (me + k) % members
-            copy = pltpu.make_async_remote_copy(
-                src_ref=block_of(sources[n], peer),
-                dst_ref=targets[n].at[me],
-                send_sem=send_sems.at[n, k],
-                recv_sem=recv_sems.at[n, k],
-                device_id={"rve": peer},
-                device_id_type=MESH,
+            copies.append(
+                pltpu.make_async_remote_copy(
+                    src_ref=source,
+                    dst_ref=target.at[me],
+                    send_sem=member_send.at[stage, k],
+                    recv_sem=member_recv.at[stage, k],
+                    device_id={"rve": (me + k) % members},
+                    device_id_type=MESH,
+                )
             )
-            copy.start()
-            copies.append(copy)
-        local = pltpu.make_async_copy(
-            block_of(sources[n], me), targets[n].at[me], local_sems.at[n]
-        )
-        local.start()
-        copies.append(local)
-    for copy in copies:
+            copies[-1].start()
+        return copies
+
+    def to_groups(stage, source, target):
+        target[mine] = source[mine]
+        copies = []
+        for k in range(1, groups):
+            peer = (mine + k) % groups
+            copies.append(
+                pltpu.make_async_remote_copy(
+                    src_ref=source.at[peer],
+                    dst_ref=target.at[mine],
+                    send_sem=group_send.at[stage, k],
+                    recv_sem=group_recv.at[stage, k],
+                    device_id={"grp": peer},
+                    device_id_type=MESH,
+                )
+            )
+            copies[-1].start()
+        return copies
+
+    def member_totals(gathered, target):
+        for g in range(groups):
+            total = gathered[0, g]
+            for r in range(1, members):
+                total = total + gathered[r, g]
+            target[g] = jnp.broadcast_to(jnp.sum(total, axis=1, keepdims=True), (8, 128))
+
+    elastic_blocks = start_blocks([0, 1])
+
+    ny, nz = displacement.shape[2:]
+    for d in range(3):
+        for x in range(2):
+            extended_v[d, x + 1] = displacement[d, x]
+    for copy in layers:
         copy.wait()
-
-    def prepare(v, carry):
-        for i in range(6):
-            off_v[v, 7 * i] = off_v[v, 7 * i] + diag_v[v, i]
-        bits, speed = branch_v[v, 0], rate_v[v, 0]
-        for a in range(SLIP):
-            critical = crss_v[v, a]
-            inverse = 1.0 / critical
-            for i in range(6):
-                schmid_v[v, 6 * a + i] = schmid_v[v, 6 * a + i] * inverse
-            active = ((bits >> a) & 1).astype(jnp.float32)
-            crss_v[v, a] = active * speed * (critical * critical)
-        for p in range(points):
-            for i in range(6):
-                strain_v[v, 6 * p + i] = jnp.full((8, 128), ebar[p, i], jnp.float32)
+    for d in range(3):
+        extended_v[d, 0] = jnp.where(linear == 0, 0.0, extended_v[d, 0])
+        extended_v[d, 3] = jnp.where(linear == devices - 1, 0.0, extended_v[d, 3])
+    node_row = lax.broadcasted_iota(jnp.int32, (ny, nz), 0)
+    node_lane = lax.broadcasted_iota(jnp.int32, (ny, nz), 1)
+    position = node_row * nz + node_lane
+
+    def shift(n, carry):
+        d, x = n // 4, n % 4
+        value = extended_v[d, x]
+        for j in range(3):
+            line = value
+            if j == 0:
+                line = jnp.where(node_row == 0, 0.0, pltpu.roll(value, 1, 0))
+            if j == 2:
+                line = jnp.where(node_row == ny - 1, 0.0, pltpu.roll(value, ny - 1, 0))
+            shifted_v[3 * j, d, x] = jnp.where(node_lane == 0, 0.0, pltpu.roll(line, 1, 1))
+            shifted_v[3 * j + 1, d, x] = line
+            shifted_v[3 * j + 2, d, x] = jnp.where(
+                node_lane == nz - 1, 0.0, pltpu.roll(line, nz - 1, 1)
+            )
         return carry
 
-    points = ebar.shape[0]
-    parts = 6 * points
-    lax.fori_loop(0, members, prepare, 0)
+    lax.fori_loop(0, 12, shift, 0)
+
+    def gradient(c, k, x):
+        if k == 0:
+            return (extended_v[c, x + 2] - extended_v[c, x]) * 0.5
+        low, high = ((1, 7), (3, 5))[k - 1]
+        return (shifted_v[high, c, x + 1] - shifted_v[low, c, x + 1]) * 0.5
+
+    starts = [node[p] - me * (2 * ny * nz) for p in range(listed)]
+    found = [[None] * 6 for p in range(listed)]
+    for i, terms in enumerate(
+        [[(0, 0)], [(1, 1)], [(2, 2)], [(1, 2), (2, 1)], [(0, 2), (2, 0)], [(0, 1), (1, 0)]]
+    ):
+        for x in range(2):
+            value = gradient(*terms[0], x)
+            for term in terms[1:]:
+                value = value + gradient(*term, x)
+            for p in range(listed):
+                picked = jnp.where(position == starts[p] - x * (ny * nz), value, 0.0)
+                found[p][i] = picked if x == 0 else found[p][i] + picked
+    own_part[...] = jnp.zeros_like(own_part)
+    for i in range(6):
+        lines = [jnp.sum(found[p][i], axis=0, keepdims=True) for p in range(listed)]
+        for g in range(groups):
+            line = jnp.where(owner[0, 0] == g, lines[0], 0.0)
+            for p in range(1, listed):
+                line = line + jnp.where(owner[p, 0] == g, lines[p], 0.0)
+            own_part[g, i : i + 1, :] = line
+    strain_parts = to_members(0, own_part, all_parts)
+    slip_blocks = start_blocks([2, 3, 4, 5])
+
+    stiff_copy.wait()
+
+    def couple(o, sums):
+        i, w = o // 9, o % 9
+        out = list(sums)
+        for x in range(2):
+            window = [shifted_v[w, d, x + i] for d in range(3)]
+            for c in range(3):
+                for d in range(3):
+                    block = stiff_v[o, c, d, x].astype(jnp.float32)
+                    out[3 * x + c] = out[3 * x + c] + block * window[d]
+        return tuple(out)
+
+    zero = jnp.zeros((ny, nz), jnp.float32)
+    applied = lax.fori_loop(0, 27, couple, (zero,) * 6)
+    for x in range(2):
+        for c in range(3):
+            residual[c, x] = external[c, x] - applied[3 * x + c]
+
+    for copy in strain_parts:
+        copy.wait()
+    member_totals(all_parts, own_total)
+    for copy in to_groups(0, own_total, all_totals):
+        copy.wait()
+    for copy in elastic_blocks:
+        copy.wait()
 
     def elastic(v, strain):
         stress = []
@@ -222,25 +386,57 @@
             edge_v[now, 0, v, k : k + 1, :] = stress[k][7:8, :]
             edge_v[now, 1, v, k : k + 1, :] = stress[k][0:1, :]
 
-    def first(v, carry):
-        keep(v, 0, elastic(v, [strain_v[v, k] for k in range(parts)]))
-        return carry
-
-    lax.fori_loop(0, members, first, 0)
     following = ring_place((place + 1) % members)
     previous = ring_place((place + members - 1) % members)
+
+    def edge_copies(now, chunk):
+        planes = pl.ds(chunk * CHUNK, CHUNK)
+        return [
+            pltpu.make_async_remote_copy(
+                src_ref=edge_v.at[now, way, planes],
+                dst_ref=halo_v.at[now, way, planes],
+                send_sem=edge_send.at[now, way, chunk],
+                recv_sem=edge_recv.at[now, way, chunk],
+                device_id={"rve": following if way == 0 else previous},
+                device_id_type=MESH,
+            )
+            for way in range(2)
+        ]
+
+    def begin(chunk, carry):
+        for n in range(CHUNK):
+            v = chunk * CHUNK + n
+            for i in range(6):
+                off_v[v, 7 * i] = off_v[v, 7 * i] + diag_v[v, i]
+            strain = []
+            for p in range(points):
+                for i in range(6):
+                    value = jnp.broadcast_to(all_totals[p, i : i + 1, :], (8, 128))
+                    strain_v[v, 6 * p + i] = value
+                    strain.append(value)
+            keep(v, 0, elastic(v, strain))
+        for copy in edge_copies(0, chunk):
+            copy.start()
+        return carry
+
+    lax.fori_loop(0, members // CHUNK, begin, 0)
+    for copy in slip_blocks:
+        copy.wait()
+
+    def prepare(v, carry):
+        bits, speed = branch_v[v, 0], rate_v[v, 0]
+        for a in range(SLIP):
+            critical = crss_v[v, a]
+            inverse = 1.0 / critical
+            for i in range(6):
+                schmid_v[v, 6 * a + i] = schmid_v[v, 6 * a + i] * inverse
+            active = ((bits >> a) & 1).astype(jnp.float32)
+            crss_v[v, a] = active * speed * (critical * critical)
+        return carry
+
+    lax.fori_loop(0, members, prepare, 0)
     row = lax.broadcasted_iota(jnp.int32, (8, 128), 0)
     top, bottom = row == 0, row == 7
-
-    def edge_copy(now, way):
-        return pltpu.make_async_remote_copy(
-            src_ref=edge_v.at[now, way],
-            dst_ref=halo_v.at[now, way],
-            send_sem=edge_send.at[now, way],
-            recv_sem=edge_recv.at[now, way],
-            device_id={"rve": following if way == 0 else previous},
-            device_id_type=MESH,
-        )
 
     def slip(now, v):
         for half in range(0, points, 2):
@@ -278,47 +474,85 @@
 
     def sweep(s, carry):
         now = s % 2
-        edges = [edge_copy(now, way) for way in range(2)]
-        for copy in edges:
-            copy.start()
 
         def slip_plane(v, inner):
             slip(now, v)
             return inner
 
-        def advance_plane(v, inner):
-            advance(now, v)
+        def advance_planes(chunk, inner):
+            for copy in edge_copies(now, chunk):
+                copy.wait()
+            for n in range(CHUNK):
+                advance(now, chunk * CHUNK + n)
+
+            @pl.when(s < SWEEPS - 1)
+            def _():
+                for copy in edge_copies(1 - now, chunk):
+                    copy.start()
+
             return inner
 
         lax.fori_loop(0, members, slip_plane, 0)
-        for copy in edges:
-            copy.wait()
-        lax.fori_loop(0, members, advance_plane, 0)
+        lax.fori_loop(0, members // CHUNK, advance_planes, 0)
         return carry
 
     lax.fori_loop(0, SWEEPS, sweep, 0)
     last = SWEEPS % 2
-    for k in range(parts):
-        total = stress_v[last, 0, k]
-        for v in range(1, members):
-            total = total + stress_v[last, v, k]
-        out[k] = total
-
-
-def volume_sums(ebar, diag, off, schmid, crss, branch, rate):
-    members = lax.axis_size("rve")
-    points = ebar.shape[0]
+    own_sum[...] = jnp.zeros_like(own_sum)
+    for p in range(points):
+        for i in range(6):
+            total = stress_v[last, 0, 6 * p + i]
+            for v in range(1, members):
+                total = total + stress_v[last, v, 6 * p + i]
+            own_sum[p, i : i + 1, :] = jnp.sum(total, axis=0, keepdims=True)
+    for copy in to_members(1, own_sum, all_sums):
+        copy.wait()
+    member_totals(all_sums, own_back)
+    for copy in to_groups(1, own_back, all_back):
+        copy.wait()
+    voxels = members * 8 * members * 128
+    for p in range(listed):
+        value = jnp.where(owner[p, 0] == 0, all_back[0], 0.0)
+        for g in range(1, groups):
+            value = value + jnp.where(owner[p, 0] == g, all_back[g], 0.0)
+        value = value / voxels
+        point_stress[p] = value
+        for c in range(3):
+            force = load[p, 6 * c] * value[0:1, :]
+            for j in range(1, 6):
+                force = force + load[p, 6 * c + j] * value[j : j + 1, :]
+            for x in range(2):
+                here = position == starts[p] - x * (ny * nz)
+                residual[c, x] = residual[c, x] - jnp.where(here, force, 0.0)
+
+
+def in_one_kernel(mesh_sizes, displacement, stiffness, external, node, owner, load, *volume):
+    groups, members = mesh_sizes
+    parts = 6 * groups
     any_space = pl.BlockSpec(memory_space=pl.ANY)
+    vector = pl.BlockSpec(memory_space=pltpu.VMEM)
+    scalar = pl.BlockSpec(memory_space=pltpu.SMEM)
 
     def held(count, dtype=jnp.float32):
         return pltpu.VMEM((members, count, 8, 128), dtype)
 
-    parts = 6 * points
-    sums = pl.pallas_call(
-        functools.partial(volume_kernel, members),
-        out_shape=jax.ShapeDtypeStruct((parts, 8, 128), jnp.float32),
-        in_specs=[pl.BlockSpec(memory_space=pltpu.SMEM)] + [any_space] * 6,
-        out_specs=pl.BlockSpec(memory_space=pltpu.VMEM),
+    def sems(*shape):
+        return pltpu.SemaphoreType.DMA(shape)
+
+    extent = displacement.shape[2:]
+    small = pltpu.VMEM((groups, 8, 128), jnp.float32)
+    gathered = pltpu.VMEM((members, groups, 8, 128), jnp.float32)
+    edges = pltpu.VMEM((2, 2, members, parts, 128), jnp.float32)
+    chunks = members // CHUNK
+    diag, off, schmid, crss, branch, rate = volume
+    residual, stress = pl.pallas_call(
+        functools.partial(volume_kernel, members, groups),
+        out_shape=(
+            jax.ShapeDtypeStruct(external.shape, jnp.float32),
+            jax.ShapeDtypeStruct((node.shape[0], 8, 128), jnp.float32),
+        ),
+        in_specs=[vector, any_space, vector] + [scalar] * 3 + [any_space] * 6,
+        out_specs=(vector, vector),
         scratch_shapes=[
             held(6),
             held(36),
@@ -328,22 +562,42 @@
             held(1),
             held(parts),
             pltpu.VMEM((2, members, parts, 8, 128), jnp.float32),
-            pltpu.VMEM((2, 2, members, parts, 128), jnp.float32),
-            pltpu.VMEM((2, 2, members, parts, 128), jnp.float32),
-            pltpu.SemaphoreType.DMA((6, members)),
-            pltpu.SemaphoreType.DMA((6, members)),
-            pltpu.SemaphoreType.DMA((6,)),
-            pltpu.SemaphoreType.DMA((2, 2)),
-            pltpu.SemaphoreType.DMA((2, 2)),
+            edges,
+            edges,
+            pltpu.VMEM(stiffness.shape, stiffness.dtype),
+            pltpu.VMEM((3, 4) + extent, jnp.float32),
+            pltpu.VMEM((9, 3, 4) + extent, jnp.float32),
+            small,
+            gathered,
+            small,
+            small,
+            small,
+            gathered,
+            small,
+            small,
+            sems(6, members),
+            sems(6, members),
+            sems(7),
+            sems(2, 2, chunks),
+            sems(2, 2, chunks),
+            sems(2),
+            sems(2),
+            sems(2, members),
+            sems(2, members),
+            sems(2, groups),
+            sems(2, groups),
         ],
         compiler_params=pltpu.CompilerParams(
-            collective_id=0, has_side_effects=True, vmem_limit_bytes=40 * 1024 * 1024
+            collective_id=0, has_side_effects=True, vmem_limit_bytes=48 * 1024 * 1024
         ),
         cost_estimate=pl.CostEstimate(
             flops=20 * 180 * parts * members * 1024, bytes_accessed=8 << 20, transcendentals=0
         ),
-    )(ebar, diag, off, schmid, crss, branch[None], rate[None])
-    return jnp.sum(sums, axis=(1, 2))
+    )(
+        displacement, stiffness, external, node, owner, load, diag, off, schmid, crss,
+        branch[None], rate[None],
+    )
+    return residual, stress[:, :6, 0]
 
 
 def plane_sums(ebar, moduli_diag, moduli_off, schmid, crss, branch, rate):
@@ -372,6 +626,13 @@
     branch,
     rate,
 ):
+    sizes = (lax.axis_size("grp"), lax.axis_size("rve"))
+    fits = sizes[1] == 8 and rate.shape[1:] == (1, 64, 128) and displacement.shape[1] == 2
+    if fits and point_node.shape[0] == 2:
+        return in_one_kernel(
+            sizes, displacement, stiffness, external, point_node, point_owner, point_load,
+            moduli_diag, moduli_off, schmid, crss, branch, rate,
+        )
     extended = padded_2(displacement, ((("grp", "rve"), 1),), 1, False)
     padded = jnp.pad(extended, ((0, 0), (0, 0), (1, 1), (1, 1)))
     applied = stiff_apply(stiffness, padded)
@@ -399,11 +660,7 @@
     arrived = lax.all_to_all(outgoing, "grp", split_axis=0, concat_axis=0, tiled=True)
     ebar = arrived.reshape(-1, 6).T
     voxels = members * rate.shape[1] * rate.shape[2] * rate.shape[3]
-    if members == 8 and rate.shape[1:] == (1, 64, 128):
-        local_sums = volume_sums(ebar.T, moduli_diag, moduli_off, schmid, crss, branch, rate)
-        local_sums = local_sums.reshape(-1, 6).T
-    else:
-        local_sums = plane_sums(ebar, moduli_diag, moduli_off, schmid, crss, branch, rate)
+    local_sums = plane_sums(ebar, moduli_diag, moduli_off, schmid, crss, branch, rate)
     totals = lax.psum(local_sums, "rve") / voxels
     returned = lax.all_to_all(
         jnp.transpose(totals.reshape(6, groups, capacity), (1, 2, 0)),

time: 181 us -> 106 us (0.59)
  blocking collectives: 31.1 us -> 0 us
  other arithmetic: 19.8 us -> 0 us
  starting transfers between devices: 12.6 us -> 0 us
  local copies, waits for them, and re-layouts: 19.1 us -> 11.5 us
  Pallas kernels: 94.9 us -> 93 us
    psum x2 -> x0, blocking collectives: 31.1 us -> none  [the longest x1 18.4 us: per_device(): quarter = lax.psum(partial_value, 'rve')]
    all_to_all x2 -> x0, starting transfers between devices: 8.95 us -> none  [the longest x1 5.09 us: per_device(): lax.all_to_all(jnp.transpose(totals.reshape(6, groups, capacity), (1, 2,...]
    reduce_sum x5 -> x0, other arithmetic: 8.77 us -> none  [the longest x3 6.75 us: stiff_apply(): jnp.sum(blocks[offset].astype(jnp.float32) * window[None], axis=1)]
    scatter-add x1 -> x0, other arithmetic: 4.75 us -> none  [per_device(): (external - applied).reshape(3, -1).at[:, safe_node]]
    ppermute x2 -> x0, starting transfers between devices: 3.64 us -> none  [the longest x1 2.35 us: padded_2(): before = lax.ppermute(last, axis, up)]
    unnamed x43 -> x22, local copies, waits for them, and re-layouts: 7.6 us -> 10.9 us
    another operation x2 -> x0, local copies, waits for them, and re-layouts: 2.92 us -> none  [node_strain(): jnp.stack([table[0][0], table[1][1], table[2][2], table[1][2] + table[2][...]
    gather x1 -> x0, local copies, waits for them, and re-layouts: 2.74 us -> none  [per_device(): partial_value = strain_field[:, safe_node].T * present[:, None]]
  transfers between devices with their start and end apart: 4 -> 0, of which waited for: 2 -> 0; matrix products, arithmetic and copies ran while one was open for 8% -> 0% of each run, Pallas kernels for 0% -> 0%
where the time goes in v1:
time: 106 us; the launch traced here: 105 us
  Pallas kernels  93 us (88%)
  local copies, waits for them, and re-layouts  11.5 us (11%)
    pallas_call x1, Pallas kernels, in_one_kernel(): pl.pallas_call(functools.partial(volume_kernel, members, groups), out_sha...  93 us
    unnamed x22, local copies, waits for them, and re-layouts  10.9 us

profile of v1, /device:TPU:0, one launch (start us, length us, event | category | flops | bytes accessed | tf_op | source)
XLA Modules:
  0.0 105.2 jit_solution(4449523944814290667)
XLA Ops:
  0.6 0.7 copy.15.owner
  1.4 0.0 copy-start
  1.4 1.7 %copy-done = f32[1,72,1,64,128]{4,3,2,1,0:T(8,128)S(1)} copy-done((f32[1,72,1,64,128]{4,3,2,1,0:T(8,128)S(1)}, f32[1,72,1,64,128]{4,3,2,1,0:T(8,128)}, u32[]{:S(2)}) %copy-start) | copy-done | bytes 2359320
  3.0 0.0 copy-start.1
  3.0 1.3 %copy-done.1 = f32[1,36,1,64,128]{4,3,2,1,0:T(8,128)S(1)} copy-done((f32[1,36,1,64,128]{4,3,2,1,0:T(8,128)S(1)}, f32[1,36,1,64,128]{4,3,2,1,0:T(8,128)}, u32[]{:S(2)}) %copy-start.1) | copy-done | bytes 1179672
  4.3 0.0 copy-start.2
  4.3 1.0 copy-done.2
  5.3 0.0 copy-start.3
  5.3 0.9 copy-done.3
  6.2 0.0 copy-start.4
  6.2 0.9 copy-done.4
  7.1 0.0 copy-start.5
  7.1 0.9 copy-done.5
  8.0 0.0 copy-start.6
  8.0 0.8 copy-done.6
  8.8 0.0 copy-start.7
  8.8 0.8 copy-done.7
  9.5 0.0 copy-start.8
  9.5 0.7 copy-done.8
  10.2 0.0 copy-start.9
  10.2 0.7 copy-done.9
  10.9 93.0 %shard_map.131 = (f32[3,2,32,128]{3,2,1,0:T(8,128)S(1)}, f32[2,8,128]{2,1,0:T(8,128)S(1)}) custom-call(f32[3,2,32,128]{3,2,1,0:T(8,128)S(1)} %copy-done.4, bf16[27,3,3,2,32,128]{5,4,3,2,1,0:T(8,128)(2,1)} %stiffness.1, f32[3,2,32,128]{3,2,1,0:T(8,128)S(1)} %copy-done.5, s32[2]{0:T(128)S(1)} %copy-done.9, s32[2,1]{1,0:T(2,128)S(1)} %copy.15.owner, ...), custom_call_target="tpu_custom_call" | custom-call | flops 707788800 | bytes 8388608 | tf_op jit(solution)/shard_map/pallas_call | solution.py:548
  103.9 0.6 slice_reduce_fusion
  104.5 0.6 copy.17
Async XLA Ops:
  1.4 1.7 %copy-start = (f32[1,72,1,64,128]{4,3,2,1,0:T(8,128)S(1)}, f32[1,72,1,64,128]{4,3,2,1,0:T(8,128)}, u32[]{:S(2)}) copy-start(f32[1,72,1,64,128]{4,3,2,1,0:T(8,128)} %schmid.1) | copy-start | bytes 7077892
  3.0 1.3 %copy-start.1 = (f32[1,36,1,64,128]{4,3,2,1,0:T(8,128)S(1)}, f32[1,36,1,64,128]{4,3,2,1,0:T(8,128)}, u32[]{:S(2)}) copy-start(f32[1,36,1,64,128]{4,3,2,1,0:T(8,128)} %off.1) | copy-start | bytes 3538948
  4.3 1.0 copy-start.2
  5.3 0.9 copy-start.3
  6.2 0.9 copy-start.4
  7.1 0.9 copy-start.5
  8.0 0.8 copy-start.6
  8.8 0.8 copy-start.7
  9.5 0.7 copy-start.8
  10.2 0.7 copy-start.9

commit v2 on v1

--- a/solution.py
+++ b/solution.py
@@ -8,6 +8,7 @@
 
 MESH = pl.DeviceIdType.MESH
 CHUNK = 2
+PIECES = 4
 
 SLIP = 12
 SWEEPS = 10
@@ -139,7 +140,9 @@
     rate,
     residual,
     point_stress,
-    diag_v,
+    own_diag,
+    own_off,
+    external_v,
     off_v,
     schmid_v,
     crss_v,
@@ -178,8 +181,6 @@
     me, mine = lax.axis_index("rve"), lax.axis_index("grp")
     linear, devices = mine * members + me, groups * members
     place = ring_place(me)
-    sources = [off, diag, schmid, crss, branch, rate]
-    targets = [off_v, diag_v, schmid_v, crss_v, branch_v, rate_v]
 
     def slab_part(number):
         number = number % devices
@@ -193,6 +194,13 @@
         pl.semaphore_signal(barrier, inc=1, device_id=device, device_id_type=MESH)
     pl.semaphore_wait(barrier, len(greeted))
 
+    near = [
+        pltpu.make_async_copy(off.at[0, :, 0], own_off, local_sems.at[0]),
+        pltpu.make_async_copy(diag.at[0, :, 0], own_diag, local_sems.at[1]),
+        pltpu.make_async_copy(displacement, extended_v.at[:, 1:3], local_sems.at[2]),
+        pltpu.make_async_copy(external, external_v, local_sems.at[3]),
+        pltpu.make_async_copy(stiffness, stiff_v, local_sems.at[4]),
+    ]
     layers = []
     for way in range(2):
         layers.append(
@@ -206,35 +214,33 @@
             )
         )
         layers[way].start()
-    stiff_copy = pltpu.make_async_copy(stiffness, stiff_v, local_sems.at[6])
-    stiff_copy.start()
-
-    def block_of(source, device):
-        rows = pl.ds(pl.multiple_of(ring_place(device) * 8, 8), 8)
-        return source.at[0, :, 0, rows, :]
-
-    def start_blocks(which):
+    for copy in near:
+        copy.start()
+
+    def start_blocks(number, source, target):
         copies = []
-        for n in which:
-            for k in range(1, members):
-                peer = (me + k) % members
-                copies.append(
-                    pltpu.make_async_remote_copy(
-                        src_ref=block_of(sources[n], peer),
-                        dst_ref=targets[n].at[me],
-                        send_sem=send_sems.at[n, k],
-                        recv_sem=recv_sems.at[n, k],
-                        device_id={"rve": peer},
-                        device_id_type=MESH,
-                    )
-                )
-                copies[-1].start()
+
+        def block_of(device):
+            rows = pl.ds(pl.multiple_of(ring_place(device) * 8, 8), 8)
+            return source.at[:, rows, :]
+
+        for k in range(1, members):
+            peer = (me + k) % members
             copies.append(
-                pltpu.make_async_copy(
-                    block_of(sources[n], me), targets[n].at[me], local_sems.at[n]
+                pltpu.make_async_remote_copy(
+                    src_ref=block_of(peer),
+                    dst_ref=target.at[me],
+                    send_sem=send_sems.at[number, k],
+                    recv_sem=recv_sems.at[number, k],
+                    device_id={"rve": peer},
+                    device_id_type=MESH,
                 )
             )
             copies[-1].start()
+        copies.append(
+            pltpu.make_async_copy(block_of(me), target.at[me], local_sems.at[5 + number])
+        )
+        copies[-1].start()
         return copies
 
     def to_members(stage, source, target):
@@ -279,12 +285,17 @@
                 total = total + gathered[r, g]
             target[g] = jnp.broadcast_to(jnp.sum(total, axis=1, keepdims=True), (8, 128))
 
-    elastic_blocks = start_blocks([0, 1])
+    weight_blocks = start_blocks(0, crss.at[0, :, 0], crss_v)
+    weight_blocks += start_blocks(1, branch.at[0, :, 0], branch_v)
+    weight_blocks += start_blocks(2, rate.at[0, :, 0], rate_v)
+    near[0].wait()
+    near[1].wait()
+    for i in range(6):
+        own_off[7 * i] = own_off[7 * i] + own_diag[i]
+    elastic_blocks = start_blocks(3, own_off, off_v)
 
     ny, nz = displacement.shape[2:]
-    for d in range(3):
-        for x in range(2):
-            extended_v[d, x + 1] = displacement[d, x]
+    near[2].wait()
     for copy in layers:
         copy.wait()
     for d in range(3):
@@ -339,9 +350,16 @@
                 line = line + jnp.where(owner[p, 0] == g, lines[p], 0.0)
             own_part[g, i : i + 1, :] = line
     strain_parts = to_members(0, own_part, all_parts)
-    slip_blocks = start_blocks([2, 3, 4, 5])
-
-    stiff_copy.wait()
+    systems = SLIP // PIECES
+    slip_blocks = []
+    for n in range(PIECES):
+        which = pl.ds(6 * systems * n, 6 * systems)
+        slip_blocks.append(
+            start_blocks(4 + n, schmid.at[0, which, 0], schmid_v.at[:, which])
+        )
+
+    near[3].wait()
+    near[4].wait()
 
     def couple(o, sums):
         i, w = o // 9, o % 9
@@ -358,7 +376,7 @@
     applied = lax.fori_loop(0, 27, couple, (zero,) * 6)
     for x in range(2):
         for c in range(3):
-            residual[c, x] = external[c, x] - applied[3 * x + c]
+            residual[c, x] = external_v[c, x] - applied[3 * x + c]
 
     for copy in strain_parts:
         copy.wait()
@@ -406,8 +424,6 @@
     def begin(chunk, carry):
         for n in range(CHUNK):
             v = chunk * CHUNK + n
-            for i in range(6):
-                off_v[v, 7 * i] = off_v[v, 7 * i] + diag_v[v, i]
             strain = []
             for p in range(points):
                 for i in range(6):
@@ -420,30 +436,28 @@
         return carry
 
     lax.fori_loop(0, members // CHUNK, begin, 0)
-    for copy in slip_blocks:
+    for copy in weight_blocks:
         copy.wait()
 
-    def prepare(v, carry):
+    def prepare(v, part):
         bits, speed = branch_v[v, 0], rate_v[v, 0]
-        for a in range(SLIP):
+        for a in part:
             critical = crss_v[v, a]
             inverse = 1.0 / critical
             for i in range(6):
                 schmid_v[v, 6 * a + i] = schmid_v[v, 6 * a + i] * inverse
             active = ((bits >> a) & 1).astype(jnp.float32)
             crss_v[v, a] = active * speed * (critical * critical)
-        return carry
-
-    lax.fori_loop(0, members, prepare, 0)
+
     row = lax.broadcasted_iota(jnp.int32, (8, 128), 0)
     top, bottom = row == 0, row == 7
 
-    def slip(now, v):
+    def slip(now, v, part):
         for half in range(0, points, 2):
             pair = range(half, min(half + 2, points))
             stress = {(p, i): stress_v[now, v, 6 * p + i] for p in pair for i in range(6)}
             change = {}
-            for a in range(SLIP):
+            for a in part:
                 rows = [schmid_v[v, 6 * a + i] for i in range(6)]
                 weight = crss_v[v, a]
                 for p in pair:
@@ -453,7 +467,7 @@
                     slipped = weight * (ratio - jnp.tanh(ratio))
                     for i in range(6):
                         term = rows[i] * slipped
-                        change[p, i] = term if a == 0 else change[p, i] + term
+                        change[p, i] = term if a == part[0] else change[p, i] + term
             for p in pair:
                 for i in range(6):
                     strain_v[v, 6 * p + i] = strain_v[v, 6 * p + i] - change[p, i]
@@ -472,12 +486,8 @@
             strain.append(value)
         keep(v, 1 - now, elastic(v, strain))
 
-    def sweep(s, carry):
+    def advance_all(s):
         now = s % 2
-
-        def slip_plane(v, inner):
-            slip(now, v)
-            return inner
 
         def advance_planes(chunk, inner):
             for copy in edge_copies(now, chunk):
@@ -492,10 +502,31 @@
 
             return inner
 
-        lax.fori_loop(0, members, slip_plane, 0)
         lax.fori_loop(0, members // CHUNK, advance_planes, 0)
+
+    def sweep(s, carry):
+        def slip_plane(v, inner):
+            slip(s % 2, v, range(SLIP))
+            return inner
+
+        @pl.when(s > 0)
+        def _():
+            lax.fori_loop(0, members, slip_plane, 0)
+
+        advance_all(s)
         return carry
 
+    for n in range(PIECES):
+        for copy in slip_blocks[n]:
+            copy.wait()
+        part = range(systems * n, systems * (n + 1))
+
+        def slip_piece(v, carry, part=part):
+            prepare(v, part)
+            slip(0, v, part)
+            return carry
+
+        lax.fori_loop(0, members, slip_piece, 0)
     lax.fori_loop(0, SWEEPS, sweep, 0)
     last = SWEEPS % 2
     own_sum[...] = jnp.zeros_like(own_sum)
@@ -529,7 +560,7 @@
 def in_one_kernel(mesh_sizes, displacement, stiffness, external, node, owner, load, *volume):
     groups, members = mesh_sizes
     parts = 6 * groups
-    any_space = pl.BlockSpec(memory_space=pl.ANY)
+    far = pl.BlockSpec(memory_space=pltpu.HBM)
     vector = pl.BlockSpec(memory_space=pltpu.VMEM)
     scalar = pl.BlockSpec(memory_space=pltpu.SMEM)
 
@@ -551,10 +582,12 @@
             jax.ShapeDtypeStruct(external.shape, jnp.float32),
             jax.ShapeDtypeStruct((node.shape[0], 8, 128), jnp.float32),
         ),
-        in_specs=[vector, any_space, vector] + [scalar] * 3 + [any_space] * 6,
+        in_specs=[far] * 3 + [scalar] * 3 + [far] * 6,
         out_specs=(vector, vector),
         scratch_shapes=[
-            held(6),
+            pltpu.VMEM((6,) + rate.shape[2:], jnp.float32),
+            pltpu.VMEM((36,) + rate.shape[2:], jnp.float32),
+            pltpu.VMEM(external.shape, jnp.float32),
             held(36),
             held(72),
             held(12),
@@ -575,9 +608,9 @@
             gathered,
             small,
             small,
-            sems(6, members),
-            sems(6, members),
-            sems(7),
+            sems(4 + PIECES, members),
+            sems(4 + PIECES, members),
+            sems(9 + PIECES),
             sems(2, 2, chunks),
             sems(2, 2, chunks),
             sems(2),
@@ -588,7 +621,7 @@
             sems(2, groups),
         ],
         compiler_params=pltpu.CompilerParams(
-            collective_id=0, has_side_effects=True, vmem_limit_bytes=48 * 1024 * 1024
+            collective_id=0, has_side_effects=True, vmem_limit_bytes=56 * 1024 * 1024
         ),
         cost_estimate=pl.CostEstimate(
             flops=20 * 180 * parts * members * 1024, bytes_accessed=8 << 20, transcendentals=0

time: 106 us -> 95.9 us (0.905)
  local copies, waits for them, and re-layouts: 11.5 us -> 4.18 us
  Pallas kernels: 93 us -> 90.8 us
    unnamed x22 -> x2, local copies, waits for them, and re-layouts: 10.9 us -> 2.84 us
    pallas_call x1, Pallas kernels: 93 us -> 90.8 us  [in_one_kernel(): pl.pallas_call(functools.partial(volume_kernel, members, groups), out_sha...]
where the time goes in v2:
time: 95.9 us; the launch traced here: 95.7 us
  Pallas kernels  90.8 us (95%)
  local copies, waits for them, and re-layouts  4.18 us (4%)
    pallas_call x1, Pallas kernels, in_one_kernel(): pl.pallas_call(functools.partial(volume_kernel, members, groups), out_sha...  90.8 us
    unnamed x2, local copies, waits for them, and re-layouts  2.84 us

profile of v2, /device:TPU:0, one launch (start us, length us, event | category | flops | bytes accessed | tf_op | source)
XLA Modules:
  0.0 95.7 jit_solution(13009538586076332138)
XLA Ops:
  0.6 1.3 %copy.15.owner = s32[2,1]{1,0:T(2,128)} copy(s32[2,1]{0,1:T(1,128)} %param.16) | data formatting | bytes 16 | tf_op args[4]
  1.9 90.8 %shard_map.131 = (f32[3,2,32,128]{3,2,1,0:T(8,128)}, f32[2,8,128]{2,1,0:T(8,128)}) custom-call(f32[3,2,32,128]{3,2,1,0:T(8,128)} %displacement.1, bf16[27,3,3,2,32,128]{5,4,3,2,1,0:T(8,128)(2,1)} %stiffness.1, f32[3,2,32,128]{3,2,1,0:T(8,128)} %external.1, s32[2]{0:T(128)} %node.1, s32[2,1]{1,0:T(2,128)} %copy.15.owner, f32[2,18]{1,0:T(2,128)} %load.1, ...), custom_call_target="tpu_custom_call" | custom-call | flops 707788800 | bytes 8388608 | tf_op jit(solution)/shard_map/pallas_call | solution.py:579
  92.8 1.3 %slice_reduce_fusion = f32[2,6]{1,0:T(2,128)} fusion(f32[2,8,128]{2,1,0:T(8,128)} %get-tuple-element.5), kind=kLoop, calls=%fused_computation | loop fusion | bytes 96 | tf_op jit(solution)/shard_map/slice | solution.py:633
  94.1 1.5 %copy.17 = f32[3,2,32,128]{3,2,1,0:T(8,128)} copy(f32[3,2,32,128]{3,2,1,0:T(8,128)} %get-tuple-element.8) | data formatting | bytes 196608
